TPU v7x, 32 devices: a whole 2x2x4 slice. The times are simulated.
32 devices in a mesh: fsdp: 8 (over z, y), tp: 4 (over x, core).
Axes of the slice: x: 2, y: 2, z: 4, core: 2. Of those that a mesh axis runs over, the one named last changes fastest.
Arguments:
- gradient: bfloat16 [768, 1280], P('fsdp', 'tp'), may hold values from -6 to 6
- momentum: float32 [768, 1280], P('fsdp', 'tp'), may hold values from -6 to 6
- q_factor: float32 [4, 320, 128], P('tp', 'fsdp'), may hold values from -6 to 6
Outputs:
- momentum_out: float32 [768, 1280], P('fsdp', 'tp')
- q_out: float32 [4, 320, 128], P('tp', 'fsdp')
- update: bfloat16 [768, 1280], P('fsdp', 'tp')
All inputs are finite; a program needn't handle non-finite values.
Results may differ from a plain program's by a relative error of at most 0.001.
Values sent between devices are 32-bit elements; how exact they have to be, the bound alone decides.
A program may use at most 64 MiB of HBM per device.

v0:
```python
import jax
import jax.numpy as jnp
from jax import lax
from jax.sharding import PartitionSpec as P


def per_device(gradient, momentum, q_factor):
    high = lax.Precision.HIGHEST
    buffer = momentum + gradient.astype(jnp.float32)
    rows_here = buffer.shape[0]
    rank_width = q_factor.shape[2]
    factor_rows = q_factor.shape[1]
    total_rows = rows_here * lax.axis_size("fsdp")
    total_cols = factor_rows * lax.axis_size("fsdp") * lax.axis_size("tp")
    columns = buffer
    partial_left = jnp.dot(
        columns,
        lax.all_gather(q_factor, "fsdp", axis=1, tiled=True)[0],
        precision=high,
        preferred_element_type=jnp.float32,
    )
    left = lax.psum(partial_left, "tp")
    gram = lax.psum(
        jnp.dot(left.T, left, precision=high, preferred_element_type=jnp.float32), "fsdp"
    )
    lower = jnp.linalg.cholesky(gram)
    basis = jax.scipy.linalg.solve_triangular(lower, left.T, lower=True).T
    update_scale = jnp.sqrt(total_rows / rank_width)
    columns = buffer
    right = lax.psum_scatter(
        jnp.dot(columns.T, basis, precision=high, preferred_element_type=jnp.float32),
        "fsdp",
        scatter_dimension=0,
        tiled=True,
    )
    squares = lax.psum(jnp.sum(right * right, axis=0), ("fsdp", "tp"))
    colscale = jnp.sqrt(squares / total_cols + 1e-06)
    q_new = right / colscale
    scaled_basis = basis * colscale
    piece = lax.all_gather(q_new, "fsdp", axis=0, tiled=True)
    columns = buffer
    feedback = columns - 0.05 * jnp.dot(
        scaled_basis, piece.T, precision=high, preferred_element_type=jnp.float32
    )
    direction = update_scale * jnp.dot(
        basis, piece.T, precision=high, preferred_element_type=jnp.float32
    )
    joined = jnp.stack([feedback, direction])
    return (joined[0], q_new[None], joined[1].astype(jnp.bfloat16))


def solution(mesh):
    placed = (P("fsdp", "tp"), P("fsdp", "tp"), P("tp", "fsdp", None))
    return jax.shard_map(
        per_device,
        mesh=mesh,
        in_specs=placed,
        out_specs=(P("fsdp", "tp"), P("tp", "fsdp", None), P("fsdp", "tp")),
        check_vma=False,
    )
```

profile of v0, /device:TPU:0, one launch (start us, length us, event | category | flops | bytes accessed | tf_op | source)
XLA Modules:
  0.0 283.7 jit_solution(7394819703464729820)
XLA Ops:
  7.2 0.0 copy-start
  7.2 0.0 all-reduce.3.cloned.1.call-start
  7.2 32.7 %all_gather.6 = f32[1,320,128]{2,1,0:T(8,128)S(1)} all-gather(f32[1,40,128]{2,1,0:T(8,128)} %param.5), channel_id=1, replica_groups=mesh['fsdp'=8,'tp'=4] {'fsdp'}, dimensions={1}, use_global_device_ids=true | all-gather | bytes 184320 | tf_op jit(solution)/shard_map/all_gather | solution.py:18
  39.9 0.0 copy-done
  39.9 1.2 fusion.2
  41.1 10.5 %psum.21 = f32[96,128]{1,0:T(8,128)S(1)} all-reduce(f32[96,128]{1,0:T(8,128)S(1)} %fusion.2), channel_id=1, replica_groups=mesh['fsdp'=8,'tp'=4] {'tp'}, use_global_device_ids=true, to_apply=%region_0.0 | all-reduce | flops 12288 | bytes 98304 | tf_op jit(solution)/shard_map/psum | solution.py:22
  51.6 0.9 fusion.11
  52.5 0.0 all-reduce.3.cloned.1.call-update
  52.6 0.0 reduce-scatter.4.cloned.1.call-start
  52.6 69.7 %all-reduce.3.cloned.1.call-done = f32[128,128]{0,1:T(8,128)} async-done(((f32[128,128]{0,1:T(8,128)}), f32[128,128]{0,1:T(8,128)}) %all-reduce.3.cloned.1.call-update) | async-done | bytes 65552 | tf_op jit(solution)/shard_map/psum | solution.py:23
  122.3 0.0 copy-start.2
  122.3 1.0 copy.9
  123.4 0.0 copy-done.2
  123.4 11.7 %cholesky.16 = f32[128,128]{1,0:T(8,128)S(1)} custom-call(f32[128,128]{1,0:T(8,128)S(1)} %fusion.7), custom_call_target="Cholesky" | custom-call | tf_op jit(solution)/shard_map/jit(cholesky)/cholesky | solution.py:26
  135.1 0.6 compare_reduce_fusion
  135.8 0.7 fusion.4
  136.4 9.8 %custom-call.7 = f32[1,128,128]{1,2,0:T(8,128)S(1)} custom-call(f32[1,128,128]{2,1,0:T(8,128)S(1)} %fusion.4), custom_call_target="InvertDiagBlocksLowerTriangular" | custom-call | tf_op jit(solution)/shard_map/jit(_solve_triangular)/triangular_solve | solution.py:27
  146.3 0.0 copy-start.1
  146.3 0.2 fusion.5
  146.5 0.7 copy-done.1
  147.1 1.1 fusion.8
  148.3 0.0 reduce-scatter.4.cloned.1.call-update
  148.3 54.4 %reduce-scatter.4.cloned.1.call-done = f32[40,128]{1,0:T(8,128)} async-done(((f32[320,128]{1,0:T(8,128)}), f32[40,128]{1,0:T(8,128)}) %reduce-scatter.4.cloned.1.call-update) | async-done | bytes 20496
  202.7 0.0 copy-start.3
  202.7 0.8 multiply_reduce_fusion
  203.5 40.1 %psum.23 = f32[128]{0:T(128)S(1)} all-reduce(f32[128]{0:T(128)S(1)} %multiply_reduce_fusion), channel_id=1, replica_groups=mesh['fsdp'=8,'tp'=4] {'fsdp','tp'}, use_global_device_ids=true, to_apply=%region_6.7 | all-reduce | flops 128 | bytes 1024 | tf_op jit(solution)/shard_map/psum | solution.py:36
  243.7 0.0 copy-done.3
  243.7 30.6 %all_gather.7 = f32[320,128]{1,0:T(8,128)S(1)} all-gather(f32[40,128]{1,0:T(8,128)S(1)} %broadcast_divide_fusion), channel_id=1, replica_groups=mesh['fsdp'=8,'tp'=4] {'fsdp'}, dimensions={0}, use_global_device_ids=true | all-gather | bytes 184320 | tf_op jit(solution)/shard_map/all_gather | solution.py:40
  274.3 1.0 fusion
  275.3 0.9 fusion.1
  276.2 0.6 fusion.19
  (4 shorter events, 0.1 us)
Async XLA Ops:
  7.2 32.8 %copy-start = (f32[96,320]{1,0:T(8,128)S(1)}, f32[96,320]{1,0:T(8,128)}, u32[]{:S(2)}) copy-start(f32[96,320]{1,0:T(8,128)} %param.4) | copy-start | bytes 368644
  7.2 115.2 %all-reduce.3.cloned.1.call-start = ((), (), s32[]{:S(2)}) async-start(), calls=%async_computation.1 | async-start | bytes 131072 | tf_op jit(solution)/shard_map/psum | solution.py:23
  52.6 150.1 %reduce-scatter.4.cloned.1.call-start = ((), (), s32[]{:S(2)}) async-start(), calls=%async_computation.2 | async-start | bytes 184320
  122.3 1.0 copy-start.2
  146.3 0.9 copy-start.1
  202.7 41.0 %copy-start.3 = (f32[40,128]{1,0:T(8,128)S(1)}, f32[40,128]{1,0:T(8,128)}, u32[]{:S(2)}) copy-start(f32[40,128]{1,0:T(8,128)} %reduce-scatter.4.cloned.1.call-done) | copy-start | bytes 61444
Sparse Core Ops, SparseCore 0:
  52.7 69.6 all-reduce.2
  148.4 54.2 reduce-scatter.3
where the time goes:
time: 284 us
  waiting for transfers between devices  124 us (44%)
  blocking collectives  114 us (40%)
  other arithmetic  24.3 us (9%)
  between operations  14.1 us (5%)
  matrix products  5.31 us (2%)
    psum x1, waiting for transfers between devices, per_device(): lax.psum(jnp.dot(left.T, left, precision=high, preferred_element_type=jnp...  69.7 us
    unnamed x3, waiting for transfers between devices  54.4 us
    psum x1, blocking collectives, per_device(): squares = lax.psum(jnp.sum(right * right, axis=0), ('fsdp', 'tp'))  40.1 us
    all_gather x1, blocking collectives, per_device(): lax.all_gather(q_factor, 'fsdp', axis=1, tiled=True)[0]  32.7 us
    all_gather x1, blocking collectives, per_device(): piece = lax.all_gather(q_new, 'fsdp', axis=0, tiled=True)  30.6 us
    another operation x3, other arithmetic, per_device(): lower = jnp.linalg.cholesky(gram)  12.4 us
    psum x1, blocking collectives, per_device(): left = lax.psum(partial_left, 'tp')  10.5 us
    another operation x2, other arithmetic, per_device(): basis = jax.scipy.linalg.solve_triangular(lower, left.T, lower=True).T  10.5 us
  transfers between devices with their start and end apart: 2, of which 2 were waited for; matrix products, arithmetic and copies ran while one was open for 0% of the time, Pallas kernels for 0%

commit v1 on v0

v1 whole, which is shorter than its diff:
```python
import functools

import jax
import jax.numpy as jnp
from jax import lax
from jax.experimental import pallas as pl
from jax.experimental.pallas import tpu as pltpu
from jax.sharding import PartitionSpec as P

MESH = pl.DeviceIdType.MESH
HIGH = lax.Precision.HIGHEST
F32 = jnp.float32
BLOCK = 16


def dot(a, b, ca, cb):
    return lax.dot_general(
        a, b, (((ca,), (cb,)), ((), ())), precision=HIGH, preferred_element_type=F32
    )


def each(start, stop, body):
    if stop - start <= 8:
        for i in range(start, stop):
            body(i)
    else:
        def step(i, carry):
            body(i)
            return carry
        lax.fori_loop(start, stop, step, 0)


def sum_slots(ref, count):
    if count <= 8:
        total = ref[0]
        for i in range(1, count):
            total = total + ref[i]
        return total
    return lax.fori_loop(1, count, lambda i, s: s + ref[i], ref[0])


def factor_block(rows_a, rows_e, first):
    b, rank = rows_a.shape
    index = lax.broadcasted_iota(jnp.int32, (b, rank), 0)
    wide = jnp.stack(
        [jnp.broadcast_to(rows_a[:, first + j : first + j + 1], (b, rank)) for j in range(b)]
    )
    scale = jnp.zeros((b, rank), F32)
    for k in range(b):
        column = wide[0]
        root = lax.rsqrt(column[k : k + 1, :])
        scale = jnp.where(index == k, root, scale)
        if k < b - 1:
            factor = jnp.where(index > k, column * (root * root), 0.0)
            rows_a = rows_a - factor * rows_a[k : k + 1, :]
            rows_e = rows_e - factor * rows_e[k : k + 1, :]
            wide = wide[1:] - factor[None] * wide[1:, k : k + 1, :]
    return rows_a * scale, rows_e * scale


def factor_range(a, e, done, first, last):
    rank = a.shape[1]
    for block in range(first, last):
        at = block * BLOCK
        upper, inverse = factor_block(a[:BLOCK], e[:BLOCK], at)
        done.append(inverse)
        if at + BLOCK < rank:
            lower = upper.T[at + BLOCK :]
            change = dot(lower, jnp.concatenate([upper, inverse], axis=1), 1, 0)
            a = a[BLOCK:] - change[:, :rank]
            e = e[BLOCK:] - change[:, rank:]
    return a, e


def kernel(
    nf, nt, rows_total, cols_total, chunk,
    grad_ref, mom_ref, q_ref, mom_out, q_out, upd_out,
    buf, q_all, parts, gram, gram_in, gram_all, m_part, m_in, m_all, right_all, sq_in,
    qs, qr, ps, pr, gs, gr, hs, hr, ms, mr, fs, fr, ss, sr,
):
    f, t = lax.axis_index("fsdp"), lax.axis_index("tp")
    rows, cols = mom_ref.shape
    kr, rank = q_ref.shape[1], q_ref.shape[2]
    gq = rank // nt
    n_chunks = cols // chunk

    def fpeer(d):
        return (lax.rem(f + d, nf), t)

    def tpeer(d):
        return (f, lax.rem(t + d, nt))

    def copy(src, dst, send, recv, d, peer):
        return pltpu.make_async_remote_copy(
            src_ref=src, dst_ref=dst, send_sem=send.at[d], recv_sem=recv.at[d],
            device_id=peer, device_id_type=MESH,
        )

    def q_copy(d):
        return copy(q_ref.at[0], q_all.at[f], qs, qr, d, fpeer(d))

    def p_copy(d):
        return copy(parts.at[t], parts.at[t], ps, pr, d, tpeer(d))

    mine = pl.ds(pl.multiple_of(t * gq, 8), gq)

    def g_copy(d):
        return copy(gram.at[mine], gram_in.at[f], gs, gr, d, fpeer(d))

    def h_copy(d):
        return copy(gram_all.at[t], gram_all.at[t], hs, hr, d, tpeer(d))

    def m_copy(d):
        return copy(m_part.at[lax.rem(f + d, nf)], m_in.at[f], ms, mr, d, fpeer(d))

    def f_copy(d):
        return copy(m_all.at[f], m_all.at[f], fs, fr, d, fpeer(d))

    def s_copy(d):
        return copy(sq_in.at[t], sq_in.at[t], ss, sr, d, tpeer(d))

    def columns(body):
        if n_chunks == 1:
            body(slice(None), slice(None))
        else:
            def step(i, carry):
                at = pl.ds(pl.multiple_of(i * chunk, 128), chunk)
                body(at, at)
                return carry
            lax.fori_loop(0, n_chunks, step, 0)

    barrier = pltpu.get_barrier_semaphore()
    each(1, nf, lambda d: pl.semaphore_signal(barrier, inc=1, device_id=fpeer(d), device_id_type=MESH))
    each(1, nt, lambda d: pl.semaphore_signal(barrier, inc=1, device_id=tpeer(d), device_id_type=MESH))
    pl.semaphore_wait(barrier, nf - 1 + nt - 1)

    each(1, nf, lambda d: q_copy(d).start())
    q_all[f] = q_ref[0]
    buf[...] = mom_ref[...] + grad_ref[...].astype(F32)
    each(1, nf, lambda d: q_copy(d).wait_recv())

    if n_chunks == 1:
        parts[t] = dot(buf[...], q_all[...].reshape(cols, rank), 1, 0)
    else:
        per = chunk // kr
        def left_step(i, total):
            at = pl.ds(pl.multiple_of(i * chunk, 128), chunk)
            return total + dot(buf[:, at], q_all[pl.ds(i * per, per)].reshape(chunk, rank), 1, 0)
        parts[t] = lax.fori_loop(0, n_chunks, left_step, jnp.zeros((rows, rank), F32))
    each(1, nt, lambda d: p_copy(d).start())
    each(1, nt, lambda d: p_copy(d).wait_recv())
    left = sum_slots(parts, nt)

    gram[...] = dot(left, left, 0, 0)
    each(1, nf, lambda d: g_copy(d).start())
    gram_in[f] = gram[mine]

    if n_chunks == 1:
        m_part[...] = dot(buf[...], left, 0, 0).reshape(nf, kr, rank)
    else:
        per = chunk // kr
        def m_step(i, carry):
            at = pl.ds(pl.multiple_of(i * chunk, 128), chunk)
            m_part[pl.ds(i * per, per)] = dot(buf[:, at], left, 0, 0).reshape(per, kr, rank)
            return carry
        lax.fori_loop(0, n_chunks, m_step, 0)
    each(1, nf, lambda d: m_copy(d).start())
    m_in[f] = m_part[f]

    each(1, nf, lambda d: g_copy(d).wait_recv())
    gram_all[t] = sum_slots(gram_in, nf)
    each(1, nt, lambda d: h_copy(d).start())
    each(1, nt, lambda d: h_copy(d).wait_recv())

    a = gram_all[...].reshape(rank, rank)
    row_id = lax.broadcasted_iota(jnp.int32, (rank, rank), 0)
    col_id = lax.broadcasted_iota(jnp.int32, (rank, rank), 1)
    e = jnp.where(row_id == col_id, 1.0, 0.0).astype(F32)
    blocks = rank // BLOCK
    done = []
    a, e = factor_range(a, e, done, 0, blocks // 2)
    each(1, nf, lambda d: m_copy(d).wait_recv())
    m_all[f] = sum_slots(m_in, nf)
    each(1, nf, lambda d: f_copy(d).start())
    factor_range(a, e, done, blocks // 2, blocks)
    inverse = jnp.concatenate(done, axis=0)
    each(1, nf, lambda d: f_copy(d).wait_recv())

    basis = dot(left, inverse, 1, 1)
    if n_chunks == 1:
        right = dot(m_all[...].reshape(cols, rank), inverse, 1, 1)
        right_all[...] = right
        squares = jnp.sum(right * right, axis=0, keepdims=True)
    else:
        per = chunk // kr
        def right_step(i, total):
            at = pl.ds(pl.multiple_of(i * chunk, 128), chunk)
            right = dot(m_all[pl.ds(i * per, per)].reshape(chunk, rank), inverse, 1, 1)
            right_all[at] = right
            return total + jnp.sum(right * right, axis=0, keepdims=True)
        squares = lax.fori_loop(0, n_chunks, right_step, jnp.zeros((1, rank), F32))
    sq_in[t] = jnp.broadcast_to(squares, (8, rank))
    each(1, nt, lambda d: s_copy(d).start())

    def feedback(at, rat):
        mom_out[:, at] = buf[:, at] - 0.05 * dot(basis, right_all[rat], 1, 1)
    columns(feedback)

    each(1, nt, lambda d: s_copy(d).wait_recv())
    colscale = jnp.sqrt(sum_slots(sq_in, nt)[0:1] / cols_total + 1e-06)
    own = right_all[pl.ds(pl.multiple_of(f * kr, 8), kr)]
    q_out[0] = own / colscale
    scaled = basis * ((rows_total / rank) ** 0.5) / colscale

    def direction(at, rat):
        upd_out[:, at] = dot(scaled, right_all[rat], 1, 1).astype(jnp.bfloat16)
    columns(direction)

    for c in (q_copy, g_copy, m_copy, f_copy):
        each(1, nf, lambda d: c(d).wait_send())
    for c in (p_copy, h_copy, s_copy):
        each(1, nt, lambda d: c(d).wait_send())


def per_device(nf, nt, gradient, momentum, q_factor):
    rows, cols = momentum.shape
    kr, rank = q_factor.shape[1], q_factor.shape[2]
    chunk = 640 if cols > 640 and cols % 640 == 0 and 640 % kr == 0 else cols
    sem = pltpu.SemaphoreType.DMA
    vmem = pl.BlockSpec(memory_space=pltpu.VMEM)
    return pl.pallas_call(
        functools.partial(kernel, nf, nt, rows * nf, cols * nt, chunk),
        out_shape=(
            jax.ShapeDtypeStruct((rows, cols), F32),
            jax.ShapeDtypeStruct((1, kr, rank), F32),
            jax.ShapeDtypeStruct((rows, cols), jnp.bfloat16),
        ),
        in_specs=[vmem] * 3,
        out_specs=(vmem,) * 3,
        scratch_shapes=[
            pltpu.VMEM((rows, cols), F32),
            pltpu.VMEM((nf, kr, rank), F32),
            pltpu.VMEM((nt, rows, rank), F32),
            pltpu.VMEM((rank, rank), F32),
            pltpu.VMEM((nf, rank // nt, rank), F32),
            pltpu.VMEM((nt, rank // nt, rank), F32),
            pltpu.VMEM((nf, kr, rank), F32),
            pltpu.VMEM((nf, kr, rank), F32),
            pltpu.VMEM((nf, kr, rank), F32),
            pltpu.VMEM((cols, rank), F32),
            pltpu.VMEM((nt, 8, rank), F32),
        ]
        + [sem((nf,)), sem((nf,)), sem((nt,)), sem((nt,)), sem((nf,)), sem((nf,)), sem((nt,)), sem((nt,))]
        + [sem((nf,)), sem((nf,)), sem((nf,)), sem((nf,)), sem((nt,)), sem((nt,))],
        compiler_params=pltpu.CompilerParams(
            collective_id=0, has_side_effects=True, vmem_limit_bytes=40 * 1024 * 1024
        ),
    )(gradient, momentum, q_factor)


def solution(mesh):
    placed = (P("fsdp", "tp"), P("fsdp", "tp"), P("tp", "fsdp", None))
    return jax.shard_map(
        functools.partial(per_device, mesh.shape["fsdp"], mesh.shape["tp"]),
        mesh=mesh,
        in_specs=placed,
        out_specs=(P("fsdp", "tp"), P("tp", "fsdp", None), P("fsdp", "tp")),
        check_vma=False,
    )
```

time: 284 us -> 42.2 us (0.15)
  waiting for transfers between devices: 124 us -> 0 us
  blocking collectives: 114 us -> 0 us
  Pallas kernels: 0 us -> 36.9 us
  other arithmetic: 24.3 us -> 0 us
  between operations: 14.1 us -> 0.65 us
  matrix products: 5.31 us -> 0 us
    psum x1 -> x0, waiting for transfers between devices: 69.7 us -> none  [per_device(): lax.psum(jnp.dot(left.T, left, precision=high, preferred_element_type=jnp...]
    all_gather x2 -> x0, blocking collectives: 63.3 us -> none  [the longest x1 32.7 us: per_device(): lax.all_gather(q_factor, 'fsdp', axis=1, tiled=True)[0]]
    unnamed x3 -> x0, waiting for transfers between devices: 54.4 us -> none
    psum x2 -> x0, blocking collectives: 50.7 us -> none  [the longest x1 40.1 us: per_device(): squares = lax.psum(jnp.sum(right * right, axis=0), ('fsdp', 'tp'))]
    pallas_call x0 -> x1, Pallas kernels: none -> 36.9 us  [per_device(): pl.pallas_call(functools.partial(kernel, nf, nt, rows * nf, cols * nt, ch...]
    another operation x5 -> x0, other arithmetic: 22.9 us -> none  [the longest x3 12.4 us: per_device(): lower = jnp.linalg.cholesky(gram)]
    dot_general x5 -> x0, matrix products: 5.12 us -> none  [the longest x1 1.16 us: per_device(): jnp.dot(columns, lax.all_gather(q_factor, 'fsdp', axis=1, tiled=True)[0],...]
    unnamed x8 -> x9, local copies, waits for them, and re-layouts: 0.69 us -> 4.42 us
  transfers between devices with their start and end apart: 2 -> 0, of which waited for: 2 -> 0; matrix products, arithmetic and copies ran while one was open for 0% -> 0% of each run, Pallas kernels for 0% -> 0%
where the time goes in v1:
time: 42.2 us; the launch traced here: 41.9 us
  Pallas kernels  36.9 us (87%)
  local copies, waits for them, and re-layouts  4.42 us (10%)
  between operations  0.65 us (2%)
    pallas_call x1, Pallas kernels, per_device(): pl.pallas_call(functools.partial(kernel, nf, nt, rows * nf, cols * nt, ch...  36.9 us
    unnamed x9, local copies, waits for them, and re-layouts  4.42 us

profile of v1, /device:TPU:0, one launch (start us, length us, event | category | flops | bytes accessed | tf_op | source)
XLA Modules:
  0.0 41.9 jit_solution(4082178708339525313)
XLA Ops:
  0.6 0.0 copy-start
  0.6 0.9 %copy-done = f32[96,320]{1,0:T(8,128)S(1)} copy-done((f32[96,320]{1,0:T(8,128)S(1)}, f32[96,320]{1,0:T(8,128)}, u32[]{:S(2)}) %copy-start) | copy-done | bytes 122904
  1.5 0.0 copy-start.1
  1.5 0.9 %copy-done.1 = bf16[96,320]{1,0:T(8,128)(2,1)S(1)} copy-done((bf16[96,320]{1,0:T(8,128)(2,1)S(1)}, bf16[96,320]{1,0:T(8,128)(2,1)}, u32[]{:S(2)}) %copy-start.1) | copy-done | bytes 61464
  2.4 0.0 copy-start.2
  2.4 0.7 %copy-done.2 = f32[1,40,128]{2,1,0:T(8,128)S(1)} copy-done((f32[1,40,128]{2,1,0:T(8,128)S(1)}, f32[1,40,128]{2,1,0:T(8,128)}, u32[]{:S(2)}) %copy-start.2) | copy-done | bytes 20504
  3.2 36.9 %shard_map.58 = (f32[96,320]{1,0:T(8,128)S(1)}, f32[1,40,128]{2,1,0:T(8,128)S(1)}, bf16[96,320]{1,0:T(8,128)(2,1)S(1)}) custom-call(bf16[96,320]{1,0:T(8,128)(2,1)S(1)} %copy-done.1, f32[96,320]{1,0:T(8,128)S(1)} %copy-done, f32[1,40,128]{2,1,0:T(8,128)S(1)} %copy-done.2), custom_call_target="tpu_custom_call" | custom-call | tf_op jit(solution)/shard_map/pallas_call | solution.py:231
  40.0 0.7 %copy.9 = f32[96,320]{1,0:T(8,128)} copy(f32[96,320]{1,0:T(8,128)S(1)} %get-tuple-element.6) | data formatting | bytes 245760
  40.7 0.6 %copy.10 = f32[1,40,128]{2,1,0:T(8,128)} copy(f32[1,40,128]{2,1,0:T(8,128)S(1)} %get-tuple-element.7) | data formatting | bytes 40960
  41.3 0.6 %copy.11 = bf16[96,320]{1,0:T(8,128)(2,1)} copy(bf16[96,320]{1,0:T(8,128)(2,1)S(1)} %get-tuple-element.8) | data formatting | bytes 122880
Async XLA Ops:
  0.6 0.9 %copy-start = (f32[96,320]{1,0:T(8,128)S(1)}, f32[96,320]{1,0:T(8,128)}, u32[]{:S(2)}) copy-start(f32[96,320]{1,0:T(8,128)} %mom_ref.1) | copy-start | bytes 368644
  1.5 0.9 %copy-start.1 = (bf16[96,320]{1,0:T(8,128)(2,1)S(1)}, bf16[96,320]{1,0:T(8,128)(2,1)}, u32[]{:S(2)}) copy-start(bf16[96,320]{1,0:T(8,128)(2,1)} %grad_ref.1) | copy-start | bytes 184324
  2.4 0.7 %copy-start.2 = (f32[1,40,128]{2,1,0:T(8,128)S(1)}, f32[1,40,128]{2,1,0:T(8,128)}, u32[]{:S(2)}) copy-start(f32[1,40,128]{2,1,0:T(8,128)} %q_ref.1) | copy-start | bytes 61444

commit v2 on v1

--- a/solution.py
+++ b/solution.py
@@ -58,6 +58,13 @@
     return rows_a * scale, rows_e * scale
 
 
+def split(x):
+    high = x.astype(jnp.bfloat16)
+    rest = x - high.astype(F32)
+    mid = rest.astype(jnp.bfloat16)
+    return high, mid, (rest - mid.astype(F32)).astype(jnp.bfloat16)
+
+
 def factor_range(a, e, done, first, last):
     rank = a.shape[1]
     for block in range(first, last):
@@ -65,8 +72,13 @@
         upper, inverse = factor_block(a[:BLOCK], e[:BLOCK], at)
         done.append(inverse)
         if at + BLOCK < rank:
-            lower = upper.T[at + BLOCK :]
-            change = dot(lower, jnp.concatenate([upper, inverse], axis=1), 1, 0)
+            h, m, l = split(jnp.concatenate([upper, inverse], axis=1))
+            hu, mu, lu = h[:, :rank], m[:, :rank], l[:, :rank]
+            lhs = jnp.concatenate([hu, hu, mu, mu, hu, lu], axis=0)
+            rhs = jnp.concatenate([h, m, h, m, l, h], axis=0)
+            change = lax.dot_general(
+                lhs, rhs, (((0,), (0,)), ((), ())), preferred_element_type=F32
+            )[at + BLOCK :]
             a = a[BLOCK:] - change[:, :rank]
             e = e[BLOCK:] - change[:, rank:]
     return a, e
@@ -74,9 +86,9 @@
 
 def kernel(
     nf, nt, rows_total, cols_total, chunk,
-    grad_ref, mom_ref, q_ref, mom_out, q_out, upd_out,
-    buf, q_all, parts, gram, gram_in, gram_all, m_part, m_in, m_all, right_all, sq_in,
-    qs, qr, ps, pr, gs, gr, hs, hr, ms, mr, fs, fr, ss, sr,
+    grad_hbm, mom_hbm, q_ref, mom_out, q_out, scaled_out, right_all,
+    grad_ref, mom_ref, buf, q_all, parts, gram, gram_in, gram_all, m_part, m_in, m_all, sq_in,
+    qs, qr, ps, pr, gs, gr, hs, hr, ms, mr, fs, fr, ss, sr, local,
 ):
     f, t = lax.axis_index("fsdp"), lax.axis_index("tp")
     rows, cols = mom_ref.shape
@@ -129,14 +141,23 @@
                 return carry
             lax.fori_loop(0, n_chunks, step, 0)
 
+    grad_copy = pltpu.make_async_copy(grad_hbm, grad_ref, local.at[0])
+    mom_copy = pltpu.make_async_copy(mom_hbm, mom_ref, local.at[1])
+    own_copy = pltpu.make_async_copy(q_ref.at[0], q_all.at[f], local.at[2])
+    own_copy.start()
+    mom_copy.start()
+    grad_copy.start()
+
     barrier = pltpu.get_barrier_semaphore()
     each(1, nf, lambda d: pl.semaphore_signal(barrier, inc=1, device_id=fpeer(d), device_id_type=MESH))
     each(1, nt, lambda d: pl.semaphore_signal(barrier, inc=1, device_id=tpeer(d), device_id_type=MESH))
     pl.semaphore_wait(barrier, nf - 1 + nt - 1)
 
     each(1, nf, lambda d: q_copy(d).start())
-    q_all[f] = q_ref[0]
+    mom_copy.wait()
+    grad_copy.wait()
     buf[...] = mom_ref[...] + grad_ref[...].astype(F32)
+    own_copy.wait()
     each(1, nf, lambda d: q_copy(d).wait_recv())
 
     if n_chunks == 1:
@@ -170,6 +191,9 @@
     each(1, nf, lambda d: g_copy(d).wait_recv())
     gram_all[t] = sum_slots(gram_in, nf)
     each(1, nt, lambda d: h_copy(d).start())
+    each(1, nf, lambda d: m_copy(d).wait_recv())
+    m_all[f] = sum_slots(m_in, nf)
+    each(1, nf, lambda d: f_copy(d).start())
     each(1, nt, lambda d: h_copy(d).wait_recv())
 
     a = gram_all[...].reshape(rank, rank)
@@ -179,9 +203,6 @@
     blocks = rank // BLOCK
     done = []
     a, e = factor_range(a, e, done, 0, blocks // 2)
-    each(1, nf, lambda d: m_copy(d).wait_recv())
-    m_all[f] = sum_slots(m_in, nf)
-    each(1, nf, lambda d: f_copy(d).start())
     factor_range(a, e, done, blocks // 2, blocks)
     inverse = jnp.concatenate(done, axis=0)
     each(1, nf, lambda d: f_copy(d).wait_recv())
@@ -210,16 +231,34 @@
     colscale = jnp.sqrt(sum_slots(sq_in, nt)[0:1] / cols_total + 1e-06)
     own = right_all[pl.ds(pl.multiple_of(f * kr, 8), kr)]
     q_out[0] = own / colscale
-    scaled = basis * ((rows_total / rank) ** 0.5) / colscale
-
-    def direction(at, rat):
-        upd_out[:, at] = dot(scaled, right_all[rat], 1, 1).astype(jnp.bfloat16)
-    columns(direction)
+    scaled_out[...] = basis * ((rows_total / rank) ** 0.5) / colscale
 
     for c in (q_copy, g_copy, m_copy, f_copy):
         each(1, nf, lambda d: c(d).wait_send())
     for c in (p_copy, h_copy, s_copy):
         each(1, nt, lambda d: c(d).wait_send())
+
+
+def finish(chunk, mom_ref, q_ref, scaled_ref, right_ref, mom_out, q_out, upd_out, upd, sem):
+    mom_copy = pltpu.make_async_copy(mom_ref, mom_out, sem.at[0])
+    q_copy = pltpu.make_async_copy(q_ref, q_out, sem.at[1])
+    mom_copy.start()
+    q_copy.start()
+    scaled = scaled_ref[...]
+    cols = upd.shape[1]
+    if cols == chunk:
+        upd[...] = dot(scaled, right_ref[...], 1, 1).astype(jnp.bfloat16)
+    else:
+        def step(i, carry):
+            at = pl.ds(pl.multiple_of(i * chunk, 128), chunk)
+            upd[:, at] = dot(scaled, right_ref[at], 1, 1).astype(jnp.bfloat16)
+            return carry
+        lax.fori_loop(0, cols // chunk, step, 0)
+    upd_copy = pltpu.make_async_copy(upd, upd_out, sem.at[2])
+    upd_copy.start()
+    mom_copy.wait()
+    q_copy.wait()
+    upd_copy.wait()
 
 
 def per_device(nf, nt, gradient, momentum, q_factor):
@@ -228,16 +267,20 @@
     chunk = 640 if cols > 640 and cols % 640 == 0 and 640 % kr == 0 else cols
     sem = pltpu.SemaphoreType.DMA
     vmem = pl.BlockSpec(memory_space=pltpu.VMEM)
-    return pl.pallas_call(
+    hbm = pl.BlockSpec(memory_space=pl.ANY)
+    mom, q_new, scaled, right = pl.pallas_call(
         functools.partial(kernel, nf, nt, rows * nf, cols * nt, chunk),
         out_shape=(
             jax.ShapeDtypeStruct((rows, cols), F32),
             jax.ShapeDtypeStruct((1, kr, rank), F32),
-            jax.ShapeDtypeStruct((rows, cols), jnp.bfloat16),
+            jax.ShapeDtypeStruct((rows, rank), F32),
+            jax.ShapeDtypeStruct((cols, rank), F32),
         ),
-        in_specs=[vmem] * 3,
-        out_specs=(vmem,) * 3,
+        in_specs=[pl.BlockSpec(memory_space=pltpu.HBM)] * 3,
+        out_specs=(vmem,) * 4,
         scratch_shapes=[
+            pltpu.VMEM((rows, cols), jnp.bfloat16),
+            pltpu.VMEM((rows, cols), F32),
             pltpu.VMEM((rows, cols), F32),
             pltpu.VMEM((nf, kr, rank), F32),
             pltpu.VMEM((nt, rows, rank), F32),
@@ -247,15 +290,26 @@
             pltpu.VMEM((nf, kr, rank), F32),
             pltpu.VMEM((nf, kr, rank), F32),
             pltpu.VMEM((nf, kr, rank), F32),
-            pltpu.VMEM((cols, rank), F32),
             pltpu.VMEM((nt, 8, rank), F32),
         ]
         + [sem((nf,)), sem((nf,)), sem((nt,)), sem((nt,)), sem((nf,)), sem((nf,)), sem((nt,)), sem((nt,))]
-        + [sem((nf,)), sem((nf,)), sem((nf,)), sem((nf,)), sem((nt,)), sem((nt,))],
+        + [sem((nf,)), sem((nf,)), sem((nf,)), sem((nf,)), sem((nt,)), sem((nt,)), sem((3,))],
         compiler_params=pltpu.CompilerParams(
             collective_id=0, has_side_effects=True, vmem_limit_bytes=40 * 1024 * 1024
         ),
-    )(gradient, momentum, q_factor)
+    )(*[pltpu.with_memory_space_constraint(x, pltpu.HBM) for x in (gradient, momentum, q_factor)])
+    return pl.pallas_call(
+        functools.partial(finish, chunk),
+        out_shape=(
+            jax.ShapeDtypeStruct((rows, cols), F32),
+            jax.ShapeDtypeStruct((1, kr, rank), F32),
+            jax.ShapeDtypeStruct((rows, cols), jnp.bfloat16),
+        ),
+        in_specs=[vmem] * 4,
+        out_specs=(hbm,) * 3,
+        scratch_shapes=[pltpu.VMEM((rows, cols), jnp.bfloat16), sem((3,))],
+        compiler_params=pltpu.CompilerParams(vmem_limit_bytes=16 * 1024 * 1024),
+    )(mom, q_new, scaled, right)
 
 
 def solution(mesh):

time: 42.2 us -> 33.8 us (0.80)
  local copies, waits for them, and re-layouts: 4.42 us -> 0 us
  Pallas kernels: 36.9 us -> 33 us
    pallas_call x1, Pallas kernels: 36.9 us -> 32 us  [per_device(): pl.pallas_call(functools.partial(kernel, nf, nt, rows * nf, cols * nt, ch...]
    unnamed x9 -> x0, local copies, waits for them, and re-layouts: 4.42 us -> none
    pallas_call x0 -> x1, Pallas kernels: none -> 0.97 us  [per_device(): pl.pallas_call(functools.partial(finish, chunk), out_shape=(jax.ShapeDtyp...]
where the time goes in v2:
time: 33.8 us; the launch traced here: 33.6 us
  Pallas kernels  33 us (98%)
  between operations  0.64 us (2%)
    pallas_call x1, Pallas kernels, per_device(): pl.pallas_call(functools.partial(kernel, nf, nt, rows * nf, cols * nt, ch...  32 us
    pallas_call x1, Pallas kernels, per_device(): pl.pallas_call(functools.partial(finish, chunk), out_shape=(jax.ShapeDtyp...  0.97 us

profile of v2, /device:TPU:0, one launch (start us, length us, event | category | flops | bytes accessed | tf_op | source)
XLA Modules:
  0.0 33.6 jit_solution(7871972465264247005)
XLA Ops:
  0.6 32.0 %shard_map.58 = (f32[96,320]{1,0:T(8,128)S(1)}, f32[1,40,128]{2,1,0:T(8,128)S(1)}, f32[96,128]{1,0:T(8,128)S(1)}, f32[320,128]{1,0:T(8,128)S(1)}) custom-call(bf16[96,320]{1,0:T(8,128)(2,1)} %grad_hbm.1, f32[96,320]{1,0:T(8,128)} %mom_hbm.1, f32[1,40,128]{2,1,0:T(8,128)} %q_ref.1), custom_call_target="tpu_custom_call" | custom-call | tf_op jit(solution)/shard_map/pallas_call | solution.py:271
  32.6 1.0 %shard_map.59 = (f32[96,320]{1,0:T(8,128)}, f32[1,40,128]{2,1,0:T(8,128)}, bf16[96,320]{1,0:T(8,128)(2,1)}) custom-call(f32[96,320]{1,0:T(8,128)S(1)} %get-tuple-element.7.mom_ref, f32[1,40,128]{2,1,0:T(8,128)S(1)} %get-tuple-element.8.q_ref, f32[96,128]{1,0:T(8,128)S(1)} %get-tuple-element.9.scaled_ref, f32[320,128]{1,0:T(8,128)S(1)} %get-tuple-element.10.right_ref), custom_call_target="tpu_custom_call" | custom-call | tf_op jit(solution)/shard_map/pallas_call | solution.py:301

commit v3 on v2

--- a/solution.py
+++ b/solution.py
@@ -17,6 +17,14 @@
     return lax.dot_general(
         a, b, (((ca,), (cb,)), ((), ())), precision=HIGH, preferred_element_type=F32
     )
+
+
+def dot3(a, b):
+    h, m, _ = split(a)
+    u, v, _ = split(b)
+    def one(x, y):
+        return lax.dot_general(x, y, (((1,), (1,)), ((), ())), preferred_element_type=F32)
+    return one(h, v) + one(m, u) + one(h, u)
 
 
 def each(start, stop, body):
@@ -205,9 +213,9 @@
     a, e = factor_range(a, e, done, 0, blocks // 2)
     factor_range(a, e, done, blocks // 2, blocks)
     inverse = jnp.concatenate(done, axis=0)
+    basis = dot(left, inverse, 1, 1)
     each(1, nf, lambda d: f_copy(d).wait_recv())
 
-    basis = dot(left, inverse, 1, 1)
     if n_chunks == 1:
         right = dot(m_all[...].reshape(cols, rank), inverse, 1, 1)
         right_all[...] = right
@@ -224,7 +232,7 @@
     each(1, nt, lambda d: s_copy(d).start())
 
     def feedback(at, rat):
-        mom_out[:, at] = buf[:, at] - 0.05 * dot(basis, right_all[rat], 1, 1)
+        mom_out[:, at] = buf[:, at] - 0.05 * dot3(basis, right_all[rat])
     columns(feedback)
 
     each(1, nt, lambda d: s_copy(d).wait_recv())
@@ -247,11 +255,11 @@
     scaled = scaled_ref[...]
     cols = upd.shape[1]
     if cols == chunk:
-        upd[...] = dot(scaled, right_ref[...], 1, 1).astype(jnp.bfloat16)
+        upd[...] = dot3(scaled, right_ref[...]).astype(jnp.bfloat16)
     else:
         def step(i, carry):
             at = pl.ds(pl.multiple_of(i * chunk, 128), chunk)
-            upd[:, at] = dot(scaled, right_ref[at], 1, 1).astype(jnp.bfloat16)
+            upd[:, at] = dot3(scaled, right_ref[at]).astype(jnp.bfloat16)
             return carry
         lax.fori_loop(0, cols // chunk, step, 0)
     upd_copy = pltpu.make_async_copy(upd, upd_out, sem.at[2])

time: 33.8 us -> 33.7 us (level)
  no operation moved by 1% of the time
where the time goes in v3:
time: 33.7 us; the launch traced here: 33.5 us
  Pallas kernels  32.9 us (98%)
  between operations  0.64 us (2%)
    pallas_call x1, Pallas kernels, per_device(): pl.pallas_call(functools.partial(kernel, nf, nt, rows * nf, cols * nt, ch...  32 us
    pallas_call x1, Pallas kernels, per_device(): pl.pallas_call(functools.partial(finish, chunk), out_shape=(jax.ShapeDtyp...  0.89 us

profile of v3, /device:TPU:0, one launch (start us, length us, event | category | flops | bytes accessed | tf_op | source)
XLA Modules:
  0.0 33.5 jit_solution(5262438743329584683)
XLA Ops:
  0.6 32.0 %shard_map.58 = (f32[96,320]{1,0:T(8,128)S(1)}, f32[1,40,128]{2,1,0:T(8,128)S(1)}, f32[96,128]{1,0:T(8,128)S(1)}, f32[320,128]{1,0:T(8,128)S(1)}) custom-call(bf16[96,320]{1,0:T(8,128)(2,1)} %grad_hbm.1, f32[96,320]{1,0:T(8,128)} %mom_hbm.1, f32[1,40,128]{2,1,0:T(8,128)} %q_ref.1), custom_call_target="tpu_custom_call" | custom-call | tf_op jit(solution)/shard_map/pallas_call | solution.py:279
  32.6 0.9 %shard_map.59 = (f32[96,320]{1,0:T(8,128)}, f32[1,40,128]{2,1,0:T(8,128)}, bf16[96,320]{1,0:T(8,128)(2,1)}) custom-call(f32[96,320]{1,0:T(8,128)S(1)} %get-tuple-element.7.mom_ref, f32[1,40,128]{2,1,0:T(8,128)S(1)} %get-tuple-element.8.q_ref, f32[96,128]{1,0:T(8,128)S(1)} %get-tuple-element.9.scaled_ref, f32[320,128]{1,0:T(8,128)S(1)} %get-tuple-element.10.right_ref), custom_call_target="tpu_custom_call" | custom-call | tf_op jit(solution)/shard_map/pallas_call | solution.py:309
